TPU v7x, 32 devices: a whole 2x2x4 slice. The times are simulated.
32 devices in a mesh: seq: 16 (over z, y, x), head: 2 (over core).
Axes of the slice: x: 2, y: 2, z: 4, core: 2. Of those that a mesh axis runs over, the one named last changes fastest.
Arguments:
- tokens: bfloat16 [16384, 1024], P('seq'), may hold values from -6 to 6
- cotangent: bfloat16 [16384, 1024], P('seq'), may hold values from -6 to 6
- lengths: int32 [8], replicated, may hold values from 1024 to 8192, as said below
- packing: int32 [8], replicated, may hold values from 0 to 7, each once
- owners: int32 [2, 49], P('head'), may hold values from 0 to 63, as said below
- slot_copy: bfloat16 [128, 1024, 128], P(('seq', 'head')), may hold values from -0.1875 to 0.1875
- slot_master: float32 [128, 1024, 128], P(('seq', 'head')), may hold values from -0.1875 to 0.1875
- slot_first: float32 [128, 1024, 128], P(('seq', 'head'))
- slot_second: float32 [128, 1024, 128], P(('seq', 'head')), as said below
- basis_left: float32 [128, 1024, 1024], P(('seq', 'head')), may hold values from -1 to 1, as said below
- basis_right: float32 [128, 128, 128], P(('seq', 'head')), may hold values from -1 to 1, as said below
- norm_gains: float32 [2, 1024], replicated, may hold values from 0.25 to 1.75
- gains_first: float32 [2, 1024], replicated
- gains_second: float32 [2, 1024], replicated, as said below
- gate_down: float32 [1024, 16], replicated, may hold values from -0.1875 to 0.1875
- down_first: float32 [1024, 16], replicated
- down_second: float32 [1024, 16], replicated, as said below
- gate_up: float32 [17, 512], P(None, 'head')
- upper_first: float32 [17, 512], P(None, 'head')
- upper_second: float32 [17, 512], P(None, 'head'), as said below
- head_gain: float32 [256], replicated, may hold values from 0.25 to 1.75
- head_first: float32 [256], replicated
- head_second: float32 [256], replicated, as said below
- conv_weight: float32 [4, 2048], P(None, 'head'), may hold values from -3 to 3
- conv_first: float32 [4, 2048], P(None, 'head')
- conv_second: float32 [4, 2048], P(None, 'head'), as said below
Outputs:
- result: bfloat16 [16384, 1024], P('seq')
- input_grad: float32 [16384, 1024], P('seq')
- slot_grad: float32 [128, 1024, 128], P(('seq', 'head'))
- master_new: float32 [128, 1024, 128], P(('seq', 'head'))
- first_new: float32 [128, 1024, 128], P(('seq', 'head'))
- second_new: float32 [128, 1024, 128], P(('seq', 'head'))
- copy_new: bfloat16 [128, 1024, 128], P(('seq', 'head'))
- gains_grad: float32 [2, 1024], replicated
- gains_new: float32 [2, 1024], replicated
- gains_first_new: float32 [2, 1024], replicated
- gains_second_new: float32 [2, 1024], replicated
- down_grad: float32 [1024, 16], replicated
- down_new: float32 [1024, 16], replicated
- down_first_new: float32 [1024, 16], replicated
- down_second_new: float32 [1024, 16], replicated
- upper_grad: float32 [17, 512], P(None, 'head')
- upper_new: float32 [17, 512], P(None, 'head')
- upper_first_new: float32 [17, 512], P(None, 'head')
- upper_second_new: float32 [17, 512], P(None, 'head')
- head_grad: float32 [256], replicated
- head_new: float32 [256], replicated
- head_first_new: float32 [256], replicated
- head_second_new: float32 [256], replicated
- conv_grad: float32 [4, 2048], P(None, 'head')
- conv_new: float32 [4, 2048], P(None, 'head')
- conv_first_new: float32 [4, 2048], P(None, 'head')
- conv_second_new: float32 [4, 2048], P(None, 'head')
Inputs may be any that keep to these rules, and one draw needn't show every extreme that they name: `owners`: each row lists 49 distinct slots; slots 0 and 63 appear in every row. The lengths sum to 15872; the largest is 8192. `packing`: each sequence appears once. `basis_left`: every [1024, 1024] slice is orthogonal. `basis_right`: every [128, 128] slice is orthogonal. `slot_second`: Positive. `gains_second`: Positive. `down_second`: Positive. `upper_second`: Positive. `head_second`: Positive. `conv_second`: Positive.
All inputs are finite; a program needn't handle non-finite values.
Results may differ from a plain program's by a relative error of at most 0.0095.
The roundings to bfloat16 on the way count: a program that leaves them out, or rounds other values in their place, can miss the bound.
Values may be sent and summed in bfloat16 or wider, within the bound.
A program may use at most 256 MiB of HBM per device.

v0:
```python
import functools

import jax
import jax.numpy as jnp
from jax import lax
from jax.experimental import pallas as pl
from jax.experimental.pallas import tpu as pltpu
from jax.sharding import PartitionSpec as P

MESH = pl.DeviceIdType.MESH

DK = 128
DV = 256


highest_precision = lax.Precision.HIGHEST
norm_epsilon = 1e-06
adam_epsilon = 1e-08
gate_scale = 16.0
moment_decay = 0.5
rate_block = 0.03
rate_gains = 0.45
rate_down = 0.02
rate_upper = 0.6
rate_head = 0.5
rate_conv = 0.1


def axis_sizes(n):
    side = 1
    while (side * 2) ** 2 * 4 <= n:
        side *= 2
    return (n // (side * side), side, side)


def coords(me, sizes):
    _, rows, columns = sizes
    return [me // (rows * columns), (me // columns) % rows, me % columns]


def index_of(c, sizes):
    _, rows, columns = sizes
    return (c[0] * rows + c[1]) * columns + c[2]


def neighbour(c, sizes, ax, j):
    d = list(c)
    d[ax] = lax.rem(c[ax] + j, sizes[ax])
    return index_of(d, sizes)


def enter(n, me, mate=False):
    barrier = pltpu.get_barrier_semaphore()
    if mate:
        core = lax.axis_index("head")
        pl.semaphore_signal(barrier, inc=1, device_id={"head": 1 - core}, device_id_type=MESH)
    for j in range(1, n):
        pl.semaphore_signal(
            barrier, inc=1, device_id={"seq": lax.rem(me + j, n)}, device_id_type=MESH
        )
    pl.semaphore_wait(barrier, n - 1 + int(mate))


def remote(src, dst, send_sem, recv_sem, peer):
    return pltpu.make_async_remote_copy(
        src_ref=src,
        dst_ref=dst,
        send_sem=send_sem,
        recv_sem=recv_sem,
        device_id={"seq": peer},
        device_id_type=MESH,
    )


def build_plan(widths, parts, pieces, orders, base=0):
    total = sum(widths)
    bounds = [sum(widths[:i]) for i in range(len(widths) + 1)]
    cuts = [round(total * f) for f in (0.0,) + parts]
    plan, at = [], 0
    for i in range(pieces):
        for order, lo, hi in zip(orders, cuts[:-1], cuts[1:], strict=True):
            size = hi - lo
            left = size * (i + 1) // pieces - size * i // pieces
            while left:
                which = max(q for q in range(len(widths)) if bounds[q] <= at)
                step = min(left, bounds[which + 1] - at)
                start = at - bounds[which]
                plan.append((which, start, start + step, at + base, order, i))
                at += step
                left -= step
    return plan


def groups_of(plan):
    streams = {}
    for i, chunk in enumerate(plan):
        streams.setdefault(chunk[4], {}).setdefault(chunk[5], []).append(i)
    return streams


def spread_steps(steps, places):
    chosen = [(place, steps.pop(0)) for place in places[: len(steps)]]

    def run(t):
        for place, step in chosen:
            pl.when(t == place)(step)

    return run


FORWARD_PLACES = (1, (4,), (4,), ())
FORWARD_PIECES = 4
BACKWARD_PLACES = ((4,), (0, 6), (2, 6))
BACKWARD_PIECES = 4
MIDDLE_PIECES = 3
MIDDLE_TAKEN = 6


def gather_steps(sizes, plan, piece, outs, bw, send, recv):
    c = coords(lax.axis_index("seq"), sizes)
    most = max(sizes)

    def copies(i, k):
        which, lo, hi, at, order, _ = plan[i]
        ax = order[k]
        wide = pl.ds(lo * bw, (hi - lo) * bw)
        index = tuple(slice(None) if a in order[:k] else c[a] for a in range(3))
        index += (slice(None), wide)
        target = outs[which].at[index]
        source = target if k else piece.at[:, pl.ds(at * bw, (hi - lo) * bw)]
        return [
            remote(
                source,
                target,
                send.at[(i * 3 + k) * most + j],
                recv.at[(i * 3 + k) * most + j],
                neighbour(c, sizes, ax, j),
            )
            for j in range(1, sizes[ax])
        ]

    streams = groups_of(plan)
    longest = max(max(s) for s in streams.values()) + 1

    def step(s):
        for k in (2, 1, 0):
            for groups in streams.values():
                for i in groups.get(s - k, ()):
                    if k:
                        for copy in copies(i, k - 1):
                            copy.wait_recv()
                    for copy in copies(i, k):
                        copy.start()

    def arrived(piece_range):
        for groups in streams.values():
            for s in piece_range:
                for i in groups.get(s, ()):
                    for copy in copies(i, 2):
                        copy.wait_recv()

    def sent():
        for i in range(len(plan)):
            for k in range(3):
                for copy in copies(i, k):
                    copy.wait_send()

    return [functools.partial(step, s) for s in range(longest + 2)], arrived, sent


def scatter_scratch(sizes, plan, rows, bw, dtype, in_place=False):
    own, first, second, third = [], [], [], []
    for _, lo, hi, _, order, _ in plan:
        wide = (hi - lo) * bw
        rest = tuple(sizes[q] for q in range(3) if q != order[0])
        own.append(pltpu.VMEM(rest + (rows, wide), dtype))
        first.append(pltpu.VMEM((sizes[order[0]] - 1,) + rest + (rows, wide), dtype))
        second.append(pltpu.VMEM((sizes[order[1]], sizes[order[2]], rows, wide), dtype))
        third.append(pltpu.VMEM((sizes[order[2]], rows, wide), dtype))
    count = len(plan) * 3 * max(sizes)
    return (
        ([] if in_place else own)
        + first
        + second
        + third
        + [
            pltpu.SemaphoreType.DMA((count,)),
            pltpu.SemaphoreType.DMA((count,)),
            pltpu.SemaphoreType.DMA((len(plan),)),
        ]
    )


def scatter_steps(sizes, plan, grads, scratch, fin, bw, in_place=False):
    c = coords(lax.axis_index("seq"), sizes)
    most, count = max(sizes), len(plan)
    first, second, third = (scratch[-3 - (3 - i) * count :][:count] for i in range(3))
    send, recv, load = scratch[-3:]

    def part(i):
        which, lo, hi, _, order, _ = plan[i]
        index = tuple(c[q] if q == order[0] else slice(None) for q in range(3))
        index += (slice(None), pl.ds(lo * bw, (hi - lo) * bw))
        return grads[which].at[index]

    own = [part(i) for i in range(count)] if in_place else scratch[:count]

    def loading(i):
        return pltpu.make_async_copy(part(i), own[i], load.at[i])

    def copies(i, k):
        which, lo, hi, _, order, _ = plan[i]
        ax = order[k]
        left = sorted(set(range(3)) - set(order[:k]))
        result = []
        for j in range(1, sizes[ax]):
            there = lax.rem(c[ax] + j, sizes[ax])
            index = tuple(there if q == ax else slice(None) for q in left)
            if k == 0:
                index += (slice(None), pl.ds(lo * bw, (hi - lo) * bw))
                source, target = grads[which].at[index], first[i].at[j - 1]
            elif k == 1:
                source, target = own[i].at[index], second[i].at[j]
            else:
                source, target = second[i].at[(0,) + index], third[i].at[j]
            s = (i * 3 + k) * most + j
            result.append(
                remote(source, target, send.at[s], recv.at[s], neighbour(c, sizes, ax, j))
            )
        return result

    def combine(i, k):
        _, lo, hi, at, order, _ = plan[i]
        if k == 0 and not in_place:
            loading(i).wait()
        for copy in copies(i, k):
            copy.wait_recv()
        size = sizes[order[k]]
        if k == 0:
            outer, inner = own[i].shape[:2]

            def add(t, _):
                u, v = t // inner, t % inner
                total = own[i][u, v].astype(jnp.float32)
                for j in range(size - 1):
                    total = total + first[i][j, u, v].astype(jnp.float32)
                own[i][u, v] = total.astype(own[i].dtype)
                return 0

            lax.fori_loop(0, outer * inner, add, 0)
        elif k == 1:
            leading = sorted(set(range(3)) - {order[0]}).index(order[1]) == 0

            def add(t, _):
                total = own[i][(c[order[1]], t) if leading else (t, c[order[1]])]
                total = total.astype(jnp.float32)
                for j in range(1, size):
                    total = total + second[i][j, t].astype(jnp.float32)
                second[i][0, t] = total.astype(own[i].dtype)
                return 0

            lax.fori_loop(0, sizes[order[2]], add, 0)
        else:
            total = second[i][0, c[order[2]]].astype(jnp.float32)
            for j in range(1, size):
                total = total + third[i][j].astype(jnp.float32)
            for b in range(hi - lo):
                fin[at + b] = total[:, b * bw : (b + 1) * bw].astype(fin.dtype)

    streams = groups_of(plan)
    longest = max(max(s) for s in streams.values()) + 1

    def step(s):
        for k in range(4):
            for groups in streams.values():
                for i in groups.get(s - k, ()):
                    if k:
                        combine(i, k - 1)
                    elif not in_place:
                        loading(i).start()
                    if k < 3:
                        for copy in copies(i, k):
                            copy.start()

    def sent():
        for i in range(count):
            for k in range(3):
                for copy in copies(i, k):
                    copy.wait_send()

    return [functools.partial(step, s) for s in range(longest + 3)], sent


SPREAD = ((2, 1, 0), (1, 2, 0), (0, 1, 2))
COLLECT = ((0, 1, 2), (0, 2, 1), (2, 1, 0))
SHARES = (0.43, 0.86, 1.0)


def sum_steps(sizes, shared, x_ref, out_ref, mate, acc, bufs, send, recv):
    me, core = lax.axis_index("seq"), lax.axis_index("head")
    c = coords(me, sizes)
    most = max(sizes)
    swap = pltpu.make_async_remote_copy(
        src_ref=x_ref.at[pl.ds(0, shared)],
        dst_ref=mate,
        send_sem=send.at[0],
        recv_sem=recv.at[0],
        device_id={"head": 1 - core},
        device_id_type=MESH,
    )

    def going(step, ax):
        copies = []
        for j in range(1, sizes[ax]):
            d = list(c)
            d[ax] = lax.rem(c[ax] + j, sizes[ax])
            q = 1 + ax * most + j
            copies.append(
                remote(
                    acc.at[step], bufs.at[ax, c[ax]], send.at[q], recv.at[q], index_of(d, sizes)
                )
            )
        return copies

    def total(ax):
        value = bufs[ax, 0]
        for j in range(1, sizes[ax]):
            value = value + bufs[ax, j]
        return value

    def start(step, ax):
        bufs[ax, c[ax]] = acc[step]
        for copy in going(step, ax):
            copy.start()

    def swapped():
        swap.wait()
        acc[0, 0:shared] = x_ref[0:shared] + mate[...]
        acc[0, shared:] = x_ref[shared:]
        start(0, 2)

    def moved(step, ax):
        for copy in going(step, ax):
            copy.wait()
        if step < 2:
            acc[step + 1] = total(ax)
            start(step + 1, ax - 1)
        else:
            out_ref[...] = total(ax)

    return [
        swap.start,
        swapped,
        functools.partial(moved, 0, 2),
        functools.partial(moved, 1, 1),
        functools.partial(moved, 2, 0),
    ]


NN = (((1,), (0,)), ((), ()))
NT = (((1,), (1,)), ((), ()))
TN = (((0,), (0,)), ((), ()))
TILE = 128
LONGEST = 8192


def halves(values):
    high = values.astype(jnp.bfloat16)
    return high, (values - high.astype(jnp.float32)).astype(jnp.bfloat16)


def product(left, right, dims):
    (lh, ll), (rh, rl) = left, right
    dot = functools.partial(
        lax.dot_general, dimension_numbers=dims, preferred_element_type=jnp.float32
    )
    return dot(lh, rh) + (dot(lh, rl) + dot(ll, rh))


def running_sum(table, values):
    first = values.astype(jnp.bfloat16)
    rest = values - first.astype(jnp.float32)
    second, third = halves(rest)
    dot = functools.partial(
        lax.dot_general, dimension_numbers=NN, preferred_element_type=jnp.float32
    )
    return dot(table, first) + (dot(table, second) + dot(table, third))


def sigmoid(values):
    return 1.0 / (1.0 + jnp.exp(-values))


def chain_tools(n, sizes, forward, mine, bufs, send, recv, result):
    me = lax.axis_index("seq")
    c = coords(me, sizes)
    pieces = mine.shape[0]
    across, along, before, held = bufs
    most = max(sizes)
    state = pl.ds(0, TILE)
    decay = pl.ds(TILE, 1)

    def peers(ax):
        return [j for j in range(1, sizes[ax])]

    def to(ax, j):
        d = list(c)
        d[ax] = lax.rem(c[ax] + j, sizes[ax])
        return index_of(d, sizes)

    def line(buf, source, ax, j, p, base):
        s = base + j * pieces + p
        return remote(source.at[p], buf.at[c[ax], p], send.at[s], recv.at[s], to(ax, j))

    place = c[0] if forward else sizes[0] - 1 - c[0]

    def hop(k, p):
        s = (2 * most + k) * pieces + p
        step = 1 if forward else -1
        d = [lax.rem(c[0] + step + sizes[0], sizes[0]), c[1], c[2]]
        return remote(
            held.at[1 + 2 * k, p], held.at[2 * k, p], send.at[s], recv.at[s], index_of(d, sizes)
        )

    def compose(first, second):
        return (second[1] * first[0] + second[0], first[1] * second[1])

    def reduce_line(buf, ax, p):
        size = sizes[ax]
        order = range(size) if forward else range(size - 1, -1, -1)
        prefix = (jnp.zeros((TILE, TILE), jnp.float32), jnp.ones((1, TILE), jnp.float32))
        total = None
        for i in order:
            item = (buf[i, p, state], buf[i, p, decay])
            longer = compose(prefix, item)
            take = (i < c[ax]) if forward else (i > c[ax])
            prefix = tuple(jnp.where(take, a, b) for a, b in zip(longer, prefix, strict=True))
            total = item if total is None else compose(total, item)
        return prefix, total

    def start_x():
        for p in range(pieces):
            across[c[2], p] = mine[p]
            for j in peers(2):
                line(across, mine, 2, j, p, 0).start()

    def start_y():
        for p in range(pieces):
            for j in peers(2):
                line(across, mine, 2, j, p, 0).wait_recv()
            prefix, total = reduce_line(across, 2, p)
            before[p, state], before[p, decay] = prefix
            held[4, p, state], held[4, p, decay] = total
            held[4, p, pl.ds(TILE + 1, 7)] = jnp.zeros((7, TILE), jnp.float32)
            along[c[1], p] = held[4, p]
            for j in peers(1):
                line(along, held.at[4], 1, j, p, most * pieces).start()

    def start_z():
        for p in range(pieces):
            for j in peers(1):
                line(along, held.at[4], 1, j, p, most * pieces).wait_recv()
            prefix, total = reduce_line(along, 1, p)
            own = (before[p, state], before[p, decay])
            before[p, state], before[p, decay] = compose(prefix, own)
            held[1, p, state], held[1, p, decay] = total
            held[1, p, pl.ds(TILE + 1, 7)] = jnp.zeros((7, TILE), jnp.float32)

            @pl.when(place < sizes[0] - 1)
            def _():
                hop(0, p).start()

    def pass_z():
        @pl.when(place > 0)
        def _():
            for p in range(pieces):
                hop(0, p).wait_recv()

                @pl.when(place < sizes[0] - 1)
                def _():
                    got = (held[0, p, state], held[0, p, decay])
                    item = (held[1, p, state], held[1, p, decay])
                    held[3, p, state], held[3, p, decay] = compose(got, item)
                    held[3, p, pl.ds(TILE + 1, 7)] = jnp.zeros((7, TILE), jnp.float32)
                    hop(1, p).start()

    def finish():
        for p in range(pieces):

            @pl.when(place == 0)
            def _():
                result[p] = before[p, state]

            @pl.when(place == 1)
            def _():
                result[p] = before[p, decay] * held[0, p, state] + before[p, state]

            @pl.when(place > 1)
            def _():
                hop(1, p).wait_recv()
                result[p] = before[p, decay] * held[2, p, state] + before[p, state]

            for j in peers(2):
                line(across, mine, 2, j, p, 0).wait_send()
            for j in peers(1):
                line(along, held.at[4], 1, j, p, most * pieces).wait_send()

        @pl.when(place < sizes[0] - 1)
        def _():
            for p in range(pieces):
                hop(0, p).wait_send()

        @pl.when((place > 0) & (place < sizes[0] - 1))
        def _():
            for p in range(pieces):
                hop(1, p).wait_send()

    return [start_x, start_y, start_z, pass_z], finish


def greet(n, sizes, extra):
    c = coords(lax.axis_index("seq"), sizes)
    barrier = pltpu.get_barrier_semaphore()
    count = 0
    for ax in range(3):
        for j in range(1, sizes[ax]):
            d = list(c)
            d[ax] = lax.rem(c[ax] + j, sizes[ax])
            pl.semaphore_signal(
                barrier, inc=1, device_id={"seq": index_of(d, sizes)}, device_id_type=MESH
            )
            count += 1
    for index in extra:
        pl.semaphore_signal(barrier, inc=1, device_id={"seq": index}, device_id_type=MESH)
        count += 1
    pl.semaphore_wait(barrier, count)


def tile_masks(rows_ref, cols_ref, c):
    row = rows_ref[pl.ds(c, 1), :]
    col = cols_ref[pl.ds(pl.multiple_of(c * TILE, TILE), TILE), 6:7]
    i = lax.broadcasted_iota(jnp.int32, (TILE, TILE), 0)
    j = lax.broadcasted_iota(jnp.int32, (TILE, TILE), 1)
    return (i >= j) & (row == col)


def forward_kernel(
    n,
    sizes,
    plan,
    ready,
    owners_ref,
    lengths_ref,
    packing_ref,
    slot_ref,
    tokens_ref,
    norm_ref,
    down_ref,
    upper_ref,
    taps_ref,
    gain_ref,
    w_in_out,
    w_up_out,
    w_out_out,
    w_down_out,
    normed_out,
    lowrank_ref,
    logits_out,
    proj_out,
    halo_ref,
    gate_out,
    conv_out,
    cum_out,
    o_out,
    u_out,
    start_out,
    cols_ref,
    rows_ref,
    normed,
    logits_ref,
    proj_ref,
    gate_ref,
    conv_ref,
    cum_ref,
    o_ref,
    u_ref,
    start_ref,
    slots,
    piece,
    w_in,
    rim,
    segs,
    act,
    state,
    prev,
    a_send,
    a_recv,
    g_send,
    g_recv,
    l_sem,
    mine,
    across,
    along,
    before,
    held,
    result,
    send,
    recv,
):
    me = lax.axis_index("seq")
    c3 = coords(me, sizes)
    length, width = tokens_ref.shape
    tiles, channels = length // TILE, proj_ref.shape[1]
    keys = logits_ref.shape[1]
    rank = down_ref.shape[0]
    heads = keys // DK
    value = DV * heads
    slots_dev, _, bw = slot_ref.shape
    rows = piece.shape[0]
    scale = DK ** (-0.5)
    enter(n, me)

    def move(j):
        p = lax.rem(me + j, n)
        return remote(
            slot_ref.at[:, pl.ds(p * rows, rows), :],
            slots.at[pl.ds(me * slots_dev, slots_dev)],
            a_send.at[j],
            a_recv.at[j],
            p,
        )

    for j in range(1, n):
        move(j).start()
    local_move = pltpu.make_async_copy(
        slot_ref.at[:, pl.ds(me * rows, rows), :],
        slots.at[pl.ds(me * slots_dev, slots_dev)],
        l_sem.at[0],
    )
    local_move.start()
    edge = remote(
        tokens_ref.at[pl.ds(length - 16, 16)],
        rim,
        a_send.at[0],
        a_recv.at[0],
        lax.rem(me + 1, n),
    )

    @pl.when(me < n - 1)
    def _():
        edge.start()

    base = me * length
    where_col = base - 8 + lax.broadcasted_iota(jnp.int32, (length + 8, 1), 0)
    lane = lax.broadcasted_iota(jnp.int32, (tiles, TILE), 1)
    where_row = base + TILE * lax.broadcasted_iota(jnp.int32, (tiles, TILE), 0) + lane
    start = jnp.int32(0)
    seg_col = jnp.zeros((length + 8, 1), jnp.float32)
    seg_row = jnp.zeros((tiles, TILE), jnp.float32)
    for q in range(lengths_ref.shape[0]):
        seg_col += (where_col >= start).astype(jnp.float32)
        seg_row += (where_row >= start).astype(jnp.float32)
        start = start + lengths_ref[packing_ref[q]]
    filled = start
    segs[...] = seg_col + (where_col >= filled).astype(jnp.float32)
    rows_ref[...] = seg_row + (where_row >= filled).astype(jnp.float32)
    lane = lax.broadcasted_iota(jnp.int32, (TILE, TILE), 1)
    for c in range(tiles):
        lo = 8 + c * TILE
        own = segs[lo : lo + TILE]
        flags = [segs[lo - 1 : lo], segs[lo + TILE - 1 : lo + TILE]]
        flags += [segs[lo - s : lo - s + TILE] for s in (1, 2, 3)]
        flags = [(other == own).astype(jnp.float32) for other in flags]
        place = base + c * TILE + lax.broadcasted_iota(jnp.int32, (TILE, 1), 0)
        flags += [None, own, (place < filled).astype(jnp.float32)]
        total = jnp.zeros((TILE, TILE), jnp.float32)
        for k, flag in enumerate(flags):
            if flag is not None:
                total = jnp.where(lane == k, flag, total)
        cols_ref[c * TILE : (c + 1) * TILE, :] = total
    cols_ref[length : length + 8, :] = jnp.zeros((8, TILE), jnp.float32)

    def norm(values):
        values = values.astype(jnp.float32)
        inverse = lax.rsqrt(jnp.mean(values * values, axis=1, keepdims=True) + norm_epsilon)
        return (values * inverse * norm_ref[...]).astype(jnp.bfloat16)

    i = lax.broadcasted_iota(jnp.int32, (TILE, TILE), 0)
    j = lax.broadcasted_iota(jnp.int32, (TILE, TILE), 1)
    lower = (i >= j).astype(jnp.bfloat16)
    down_low = down_ref[...].astype(jnp.bfloat16)
    upper = halves(upper_ref[0:rank, :])

    def gates(c, _):
        at = pl.ds(pl.multiple_of(c * TILE, TILE), TILE)
        x = norm(tokens_ref[at, :])
        normed[at, :] = x
        low = lax.dot_general(x, down_low, NT, preferred_element_type=jnp.float32)
        lowrank_ref[at, :] = low
        logits = product(halves(low), upper, NN) + upper_ref[rank : rank + 1, :]
        logits_ref[at, :] = logits
        gate = jnp.minimum(logits, 0.0) - jnp.log1p(jnp.exp(-jnp.abs(logits)))
        cum_ref[at, :] = running_sum(lower, gate * (1.0 / gate_scale))
        return 0

    lax.fori_loop(0, tiles, gates, 0)
    flushes = []

    def flush(source, target):
        copy = pltpu.make_async_copy(source, target, l_sem.at[6 + len(flushes)])
        copy.start()
        flushes.append(copy)

    flush(normed, normed_out)
    flush(logits_ref, logits_out)
    flush(cum_ref, cum_out)

    @pl.when(me > 0)
    def _():
        edge.wait_recv()

    @pl.when(me == 0)
    def _():
        rim[...] = jnp.zeros_like(rim)

    rim[...] = norm(rim[...])

    local_move.wait()
    for j in range(1, n):
        move(j).wait()
    for b in range(owners_ref.shape[1]):
        piece[:, b * bw : (b + 1) * bw] = slots[owners_ref[0, b]]
    outs = (w_in, w_up_out, w_out_out, w_down_out)
    offset, owns = 0, []
    for q, out in enumerate(outs):
        columns = out.shape[4]
        owns.append(
            pltpu.make_async_copy(
                piece.at[:, pl.ds(offset, columns)],
                out.at[c3[0], c3[1], c3[2]],
                l_sem.at[1 + q],
            )
        )
        offset += columns
    for copy in owns:
        copy.start()
    steps, arrived, sent = gather_steps(sizes, plan, piece, outs, bw, g_send, g_recv)
    steps[0]()
    for copy in owns:
        copy.wait()
    for step in steps[1 : ready + 2]:
        step()
    arrived(range(ready))
    rest = list(steps[ready + 2 :])
    flush(w_in, w_in_out)

    for step in rest[: FORWARD_PLACES[0]]:
        step()
    del rest[: FORWARD_PLACES[0]]

    def project(r, _):
        at = pl.ds(pl.multiple_of(r * 256, 256), 256)
        x = normed[at, :]
        for lo in range(0, w_in.shape[4], 512):
            part = lax.dot_general(
                x,
                w_in[:, :, :, :, lo : lo + 512].reshape(width, 512),
                NN,
                preferred_element_type=jnp.float32,
            )
            if lo < channels:
                proj_ref[at, lo : lo + 512] = part.astype(proj_ref.dtype)
            else:
                gate_ref[at, lo - channels : lo - channels + 512] = part
        return 0

    lax.fori_loop(0, length // 256, project, 0)
    for lo in range(0, channels, 512):
        halo_ref[:, lo : lo + 512] = lax.dot_general(
            rim[...],
            w_in[:, :, :, :, lo : lo + 512].reshape(width, 512),
            NN,
            preferred_element_type=jnp.float32,
        ).astype(halo_ref.dtype)
    flush(proj_ref, proj_out)
    flush(gate_ref, gate_out)

    prev[...] = halo_ref[...]
    state[...] = jnp.zeros_like(state)
    mine[...] = jnp.zeros_like(mine)
    for p in range(mine.shape[0]):
        mine[p, TILE : TILE + 1] = jnp.ones((1, TILE), jnp.float32)
    run = spread_steps(rest, FORWARD_PLACES[1])

    def local(c, _):
        run(c)
        at = pl.ds(pl.multiple_of(c * TILE, TILE), TILE)
        for g in range(0, channels, 256):
            wide = slice(g, g + 256)
            block = jnp.concatenate(
                [prev[:, wide].astype(jnp.float32), proj_ref[at, wide].astype(jnp.float32)]
            )
            total = taps_ref[3:4, wide] * block[16:]
            for s in (1, 2, 3):
                total = total + taps_ref[3 - s : 4 - s, wide] * (
                    block[16 - s : 16 - s + TILE] * cols_ref[at, 1 + s : 2 + s]
                )
            conv_ref[at, wide] = total
            act[at, wide] = total * sigmoid(total)
        prev[...] = proj_ref[pl.ds(pl.multiple_of(c * TILE + TILE - 16, 16), 16), :]
        cum = cum_ref[at, :]
        last = cum[TILE - 1 : TILE]
        left = act[at, keys : 2 * keys] * jnp.exp(last - cum) * cols_ref[at, 1:2]
        decay = jnp.exp(last) * cols_ref[at, 0:1][TILE - 1 : TILE]
        for h in range(heads):
            kh = slice(h * DK, (h + 1) * DK)
            v = halves(act[at, 2 * keys + h * DV : 2 * keys + (h + 1) * DV])
            start_ref[c, h] = state[h]
            state[h] = state[h] * decay[:, kh] + product(v, halves(left[:, kh]), TN)
            for e in range(DV // TILE):
                p = h * (DV // TILE) + e
                mine[p, TILE : TILE + 1] = mine[p, TILE : TILE + 1] * decay[:, kh]
        return 0

    lax.fori_loop(0, tiles, local, 0)
    flush(conv_ref, conv_out)
    for h in range(heads):
        start_ref[tiles, h] = state[h]
        for e in range(DV // TILE):
            mine[h * (DV // TILE) + e, 0:TILE] = state[h, e * TILE : (e + 1) * TILE]
    stages, finish = chain_tools(
        n, sizes, True, mine, (across, along, before, held), send, recv, result
    )
    stages[0]()
    run_inside = spread_steps(rest, FORWARD_PLACES[2])

    def inside(c, _):
        for k, stage in enumerate(stages[1:]):
            pl.when(c == k + 1)(stage)
        run_inside(c)
        at = pl.ds(pl.multiple_of(c * TILE, TILE), TILE)
        cum = cum_ref[at, :]
        middle = cum[TILE // 2 - 1 : TILE // 2]
        q = act[at, 0:keys] * jnp.exp(cum - middle) * scale
        k = act[at, keys : 2 * keys] * jnp.exp(middle - cum)
        mask = tile_masks(rows_ref, cols_ref, c)
        for h in range(heads):
            kh = slice(h * DK, (h + 1) * DK)
            vh = slice(h * DV, (h + 1) * DV)
            scores = jnp.where(mask, product(halves(q[:, kh]), halves(k[:, kh]), NT), 0.0)
            v = halves(act[at, 2 * keys + h * DV : 2 * keys + (h + 1) * DV])
            o_ref[at, vh] = product(halves(scores), v, NN)
        return 0

    lax.fori_loop(0, tiles, inside, 0)
    finish()
    for h in range(heads):
        for e in range(DV // TILE):
            state[h, e * TILE : (e + 1) * TILE] = result[h * (DV // TILE) + e]

    run_outside = spread_steps(rest, FORWARD_PLACES[3])

    def outside(c, _):
        run_outside(c)
        at = pl.ds(pl.multiple_of(c * TILE, TILE), TILE)
        cum = cum_ref[at, :]
        q = act[at, 0:keys] * jnp.exp(cum) * scale * cols_ref[at, 0:1]
        decay = jnp.exp(cum[TILE - 1 : TILE]) * cols_ref[at, 0:1][TILE - 1 : TILE]
        for h in range(heads):
            kh = slice(h * DK, (h + 1) * DK)
            vh = slice(h * DV, (h + 1) * DV)
            begin = start_ref[c, h] + state[h]
            start_ref[c, h] = begin
            state[h] = state[h] * decay[:, kh]
            o = o_ref[at, vh] + product(halves(q[:, kh]), halves(begin), NT)
            o_ref[at, vh] = o
            inverse = lax.rsqrt(jnp.mean(o * o, axis=1, keepdims=True) + norm_epsilon)
            gate = gate_ref[at, vh]
            u_ref[at, vh] = (o * inverse * gain_ref[...] * (gate * sigmoid(gate))).astype(
                u_ref.dtype
            )
        return 0

    lax.fori_loop(0, tiles, outside, 0)
    for h in range(heads):
        start_ref[tiles, h] = start_ref[tiles, h] + state[h]
    flush(o_ref, o_out)
    flush(u_ref, u_out)
    flush(start_ref, start_out)
    for step in rest:
        step()
    groups = {chunk[5] for chunk in plan}
    arrived(sorted(g for g in groups if g >= ready))
    sent()
    for copy in flushes:
        copy.wait()

    @pl.when(me < n - 1)
    def _():
        edge.wait_send()


def forward(
    owners, lengths, packing, slot_copy, tokens, norm, down, upper, taps, gain, counts
):
    n = lax.axis_size("seq")
    sizes = axis_sizes(n)
    length, width = tokens.shape
    slots_dev, depth, bw = slot_copy.shape
    rows = depth // n
    keys, channels = upper.shape[1], taps.shape[1]
    heads = keys // DK
    value = heads * DV
    tiles = length // TILE
    blocks = sum(counts)
    ready = 2
    plan = build_plan(counts[:1], SHARES, ready, COLLECT)
    plan += [
        (which + 1, lo, hi, at, order, group + ready)
        for which, lo, hi, at, order, group in build_plan(
            counts[1:], SHARES, FORWARD_PIECES, COLLECT, counts[0]
        )
    ]
    f32, b16 = jnp.float32, jnp.bfloat16
    shape = jax.ShapeDtypeStruct
    vmem, anywhere = pl.BlockSpec(memory_space=pltpu.VMEM), pl.BlockSpec(memory_space=pl.ANY)
    smem = pl.BlockSpec(memory_space=pltpu.SMEM)
    kept = [
        ((length, width), b16),
        ((length, keys), f32),
        ((length, channels), b16),
        ((length, value), f32),
        ((length, channels), f32),
        ((length, keys), f32),
        ((length, value), f32),
        ((length, value), b16),
        ((tiles + 1, heads, DV, DK), f32),
    ]
    big = [shape(*k) for k in kept]
    outs = [shape(sizes + (rows, count * bw), b16) for count in counts]
    outs += [big[0], shape((length, down.shape[0]), f32), big[1], big[2]]
    outs += [shape((16, channels), b16)] + big[3:]
    outs += [shape((length + 8, TILE), f32), shape((tiles, TILE), f32)]
    specs = [anywhere] * 5 + [vmem, anywhere, anywhere, vmem] + [anywhere] * 6 + [vmem, vmem]
    most = max(sizes)
    copies = len(plan) * 3 * most
    result = pl.pallas_call(
        functools.partial(forward_kernel, n, sizes, plan, ready),
        out_shape=tuple(outs),
        in_specs=[smem] * 3 + [anywhere] + [vmem] * 6,
        out_specs=tuple(specs),
        scratch_shapes=[pltpu.VMEM(*k) for k in kept]
        + [
            pltpu.VMEM((n * slots_dev, rows, bw), b16),
            pltpu.VMEM((rows, blocks * bw), b16),
            pltpu.VMEM(sizes + (rows, counts[0] * bw), b16),
            pltpu.VMEM((16, width), b16),
            pltpu.VMEM((length + 8, 1), f32),
            pltpu.VMEM((length, channels), f32),
            pltpu.VMEM((heads, DV, DK), f32),
            pltpu.VMEM((16, channels), b16),
            pltpu.SemaphoreType.DMA((n,)),
            pltpu.SemaphoreType.DMA((n,)),
            pltpu.SemaphoreType.DMA((copies,)),
            pltpu.SemaphoreType.DMA((copies,)),
            pltpu.SemaphoreType.DMA((18,)),
        ]
        + chain_scratch(sizes, heads * DV // TILE, length),
        compiler_params=pltpu.CompilerParams(
            collective_id=1, has_side_effects=True, vmem_limit_bytes=60 << 20
        ),
    )(owners, lengths, packing, slot_copy, tokens, norm, down, upper, taps, gain)
    return [w.reshape(depth, w.shape[4]) for w in result[:4]], result[4:]


def chain_scratch(sizes, pieces, length):
    assert 2 * sizes[1] * sizes[2] * length >= LONGEST
    most = max(sizes)
    shape = (pieces, TILE + 8, TILE)
    return [
        pltpu.VMEM(shape, jnp.float32),
        pltpu.VMEM((sizes[2],) + shape, jnp.float32),
        pltpu.VMEM((sizes[1],) + shape, jnp.float32),
        pltpu.VMEM(shape, jnp.float32),
        pltpu.VMEM((5,) + shape, jnp.float32),
        pltpu.VMEM((pieces, TILE, TILE), jnp.float32),
        pltpu.SemaphoreType.DMA(((2 * most + 2) * pieces,)),
        pltpu.SemaphoreType.DMA(((2 * most + 2) * pieces,)),
    ]


def backward_kernel(
    n,
    sizes,
    plan,
    proj_in,
    halo_ref,
    conv_in,
    cum_in,
    logits_in,
    o_in,
    gate_in,
    du_in,
    start_in,
    cols_ref,
    rows_ref,
    taps_ref,
    gain_ref,
    g_up_ref,
    g_out_ref,
    dproj_out,
    dgate_out,
    dlogits_out,
    dtaps_ref,
    dgain_ref,
    early_ref,
    proj_ref,
    conv_ref,
    cum_ref,
    logits_ref,
    o_ref,
    gate_ref,
    du_ref,
    start_ref,
    dproj_ref,
    dgate_ref,
    dlogits_ref,
    t_sem,
    l_sem,
    do,
    dact,
    adjoint,
    ends,
    after,
    back,
    tail,
    mine,
    across,
    along,
    before,
    held,
    result,
    send,
    recv,
    b_sem,
    *scatter_refs,
):
    tiles, channels = proj_ref.shape[0] // TILE, proj_ref.shape[1]
    keys = cum_ref.shape[1]
    heads = keys // DK
    me = lax.axis_index("seq")
    by_tile = (
        (du_in, du_ref),
        (o_in, o_ref),
        (gate_in, gate_ref),
        (cum_in, cum_ref),
        (conv_in.at[:, pl.ds(0, keys)], conv_ref.at[:, pl.ds(0, keys)]),
    )
    rest = pl.ds(keys, channels - keys)
    whole = (
        (conv_in.at[:, rest], conv_ref.at[:, rest]),
        (start_in, start_ref),
        (proj_in, proj_ref),
        (logits_in, logits_ref),
        (dgate_ref, dgate_out),
        (dlogits_ref, dlogits_out),
        (dproj_ref, dproj_out),
    )

    def tile_load(q, c):
        at = pl.ds(pl.multiple_of(c * TILE, TILE), TILE)
        source, target = by_tile[q]
        return pltpu.make_async_copy(source.at[at], target.at[at], t_sem.at[q, c])

    def load(q):
        source, target = whole[q]
        return pltpu.make_async_copy(source, target, l_sem.at[q])

    for c in range(tiles - 1, -1, -1):
        for q in range(len(by_tile)):
            tile_load(q, c).start()
    for q in range(4):
        load(q).start()
    greet(n, sizes, (lax.rem(me + 1, n), lax.rem(me + n - 1, n)))
    steps, sent = scatter_steps(
        sizes, plan, [g_up_ref, g_out_ref], scatter_refs, early_ref, TILE
    )
    steps.pop(0)()
    run_local = spread_steps(steps, BACKWARD_PLACES[0])
    run_inside = spread_steps(steps, BACKWARD_PLACES[1])
    run_outside = spread_steps(steps, BACKWARD_PLACES[2])
    scale = DK ** (-0.5)
    i = lax.broadcasted_iota(jnp.int32, (TILE, TILE), 0)
    j = lax.broadcasted_iota(jnp.int32, (TILE, TILE), 1)
    upper = (i <= j).astype(jnp.bfloat16)
    adjoint[...] = jnp.zeros_like(adjoint)
    mine[...] = jnp.zeros_like(mine)
    dgain_ref[...] = jnp.zeros_like(dgain_ref)
    dtaps_ref[...] = jnp.zeros_like(dtaps_ref)
    for p in range(mine.shape[0]):
        mine[p, TILE : TILE + 1] = jnp.ones((1, TILE), jnp.float32)

    def local(t, _):
        run_local(t)
        c = tiles - 1 - t
        for q in range(len(by_tile)):
            tile_load(q, c).wait()
        at = pl.ds(pl.multiple_of(c * TILE, TILE), TILE)
        cum = cum_ref[at, :]
        pre = conv_ref[at, 0:keys]
        q = pre * sigmoid(pre) * jnp.exp(cum) * scale * cols_ref[at, 0:1]
        decay = jnp.exp(cum[TILE - 1 : TILE]) * cols_ref[at, 0:1][TILE - 1 : TILE]
        for h in range(heads):
            kh = slice(h * DK, (h + 1) * DK)
            vh = slice(h * DV, (h + 1) * DV)
            o = o_ref[at, vh]
            inverse = lax.rsqrt(jnp.mean(o * o, axis=1, keepdims=True) + norm_epsilon)
            gate = gate_ref[at, vh]
            sig = sigmoid(gate)
            du = du_ref[at, vh]
            unit = o * inverse
            dgate_ref[at, vh] = (
                du * (unit * gain_ref[...]) * (sig * (1.0 + gate * (1.0 - sig)))
            ).astype(dgate_ref.dtype)
            don = du * (gate * sig)
            dgain_ref[0:1] += jnp.sum(don * unit, axis=0, keepdims=True)
            scaled = gain_ref[...] * don
            grad = inverse * scaled - unit * (
                inverse * inverse * jnp.mean(scaled * o, axis=1, keepdims=True)
            )
            do[at, vh] = grad
            ends[c, h] = adjoint[h]
            adjoint[h] = adjoint[h] * decay[:, kh] + product(halves(grad), halves(q[:, kh]), TN)
            for e in range(DV // TILE):
                p = h * (DV // TILE) + e
                mine[p, TILE : TILE + 1] = mine[p, TILE : TILE + 1] * decay[:, kh]
        return 0

    lax.fori_loop(0, tiles, local, 0)
    load(4).start()
    for h in range(heads):
        for e in range(DV // TILE):
            mine[h * (DV // TILE) + e, 0:TILE] = adjoint[h, e * TILE : (e + 1) * TILE]
    stages, finish = chain_tools(
        n, sizes, False, mine, (across, along, before, held), send, recv, result
    )
    stages[0]()
    load(0).wait()
    load(1).wait()

    def inside(c, _):
        for k, stage in enumerate(stages[1:]):
            pl.when(c == k + 1)(stage)
        run_inside(c)
        at = pl.ds(pl.multiple_of(c * TILE, TILE), TILE)
        cum = cum_ref[at, :]
        middle = cum[TILE // 2 - 1 : TILE // 2]
        pre = conv_ref[at, 0 : 2 * keys]
        both = pre * sigmoid(pre)
        grow = jnp.exp(cum - middle) * scale
        fall = jnp.exp(middle - cum)
        enter_decay = jnp.exp(cum) * (scale * cols_ref[at, 0:1])
        mask = tile_masks(rows_ref, cols_ref, c)
        for h in range(heads):
            kh = slice(h * DK, (h + 1) * DK)
            vh = slice(h * DV, (h + 1) * DV)
            q = halves(both[:, kh] * grow[:, kh])
            k = halves(both[:, keys + h * DK : keys + (h + 1) * DK] * fall[:, kh])
            prev_v = conv_ref[at, 2 * keys + h * DV : 2 * keys + (h + 1) * DV]
            v = halves(prev_v * sigmoid(prev_v))
            grad = halves(do[at, vh])
            scores = halves(jnp.where(mask, product(q, k, NT), 0.0))
            dscores = halves(jnp.where(mask, product(grad, v, NT), 0.0))
            dact[at, h * DK : (h + 1) * DK] = (
                product(dscores, k, NN) * grow[:, kh]
                + product(grad, halves(start_ref[c, h]), NN) * enter_decay[:, kh]
            )
            dact[at, keys + h * DK : keys + (h + 1) * DK] = (
                product(dscores, q, TN) * fall[:, kh]
            )
            dact[at, 2 * keys + h * DV : 2 * keys + (h + 1) * DV] = product(scores, grad, TN)
        return 0

    lax.fori_loop(0, tiles, inside, 0)
    finish()
    for h in range(heads):
        for e in range(DV // TILE):
            adjoint[h, e * TILE : (e + 1) * TILE] = result[h * (DV // TILE) + e]
    after[...] = jnp.zeros_like(after)
    load(2).wait()
    load(3).wait()

    def outside(t, _):
        run_outside(t)
        c = tiles - 1 - t
        at = pl.ds(pl.multiple_of(c * TILE, TILE), TILE)
        cum = cum_ref[at, :]
        last = cum[TILE - 1 : TILE]
        remain = jnp.exp(last - cum) * cols_ref[at, 1:2]
        decay = jnp.exp(last) * cols_ref[at, 0:1][TILE - 1 : TILE]
        pre = conv_ref[at, 0 : 2 * keys]
        both = pre * sigmoid(pre)
        dkeys, edges = [], []
        for h in range(heads):
            kh = slice(h * DK, (h + 1) * DK)
            wide = slice(2 * keys + h * DV, 2 * keys + (h + 1) * DV)
            k = both[:, keys + h * DK : keys + (h + 1) * DK]
            end = ends[c, h] + adjoint[h]
            adjoint[h] = adjoint[h] * decay[:, kh]
            parts = halves(end)
            pre_v = conv_ref[at, wide]
            v = halves(pre_v * sigmoid(pre_v))
            dkeys.append(
                dact[at, keys + h * DK : keys + (h + 1) * DK]
                + product(v, parts, NN) * remain[:, kh]
            )
            dact[at, wide] += product(halves(k * remain[:, kh]), parts, NT)
            edges.append(jnp.sum(end * start_ref[c + 1, h], axis=0, keepdims=True))
        dk = jnp.concatenate(dkeys, axis=1)
        dq = dact[at, 0:keys]
        dact[at, keys : 2 * keys] = dk
        drift = both[:, 0:keys] * dq - both[:, keys:] * dk
        dl = running_sum(upper, drift) + jnp.concatenate(edges, axis=1)
        dlogits_ref[at, :] = dl * (1.0 / gate_scale) * sigmoid(-logits_ref[at, :])
        behind = jnp.where(
            c == 0,
            halo_ref[...],
            proj_ref[pl.ds(pl.multiple_of(jnp.maximum(c * TILE - 16, 0), 16), 16), :],
        )
        masks = cols_ref[pl.ds(pl.multiple_of(c * TILE, TILE), TILE + 8), :]
        for g in range(0, channels, 256):
            wide = slice(g, g + 256)
            pre = conv_ref[at, wide]
            sig = sigmoid(pre)
            dconv = dact[at, wide] * (sig * (1.0 + pre * (1.0 - sig)))
            block = jnp.concatenate(
                [
                    behind[:, g : g + 256].astype(jnp.float32),
                    proj_ref[at, wide].astype(jnp.float32),
                ]
            )
            grad = jnp.concatenate([dconv, after[:, wide]])
            total = taps_ref[3:4, wide] * dconv
            dtaps_ref[3:4, wide] += jnp.sum(dconv * block[16:], axis=0, keepdims=True)
            first = jnp.zeros((8, 256), jnp.float32)
            for s in (1, 2, 3):
                masked = grad * masks[:, 1 + s : 2 + s]
                tap = taps_ref[3 - s : 4 - s, wide]
                total = total + tap * masked[s : s + TILE]
                dtaps_ref[3 - s : 4 - s, wide] += jnp.sum(
                    masked[:TILE] * block[16 - s : 16 - s + TILE], axis=0, keepdims=True
                )
                first = first + tap * jnp.concatenate(
                    [jnp.zeros((8, 256), jnp.float32), masked[0:8]]
                )[s : s + 8]
            dproj_ref[at, wide] = total.astype(dproj_ref.dtype)
            after[:, wide] = dconv[0:8]
            back[0, :, wide] = first

            @pl.when(c == tiles - 1)
            def _():
                tail[:, wide] = total[TILE - 16 :]

        return 0

    lax.fori_loop(0, tiles, outside, 0)
    load(5).start()

    home = remote(
        back.at[0], back.at[1], b_sem.at[0], b_sem.at[1], lax.rem(me + n - 1, n)
    )

    @pl.when(me > 0)
    def _():
        home.start()

    for step in steps[:1]:
        step()

    @pl.when(me < n - 1)
    def _():
        home.wait_recv()

    @pl.when(me == n - 1)
    def _():
        back[1] = jnp.zeros(back.shape[1:], jnp.float32)

    dproj_ref[pl.ds(tiles * TILE - 16, 16), :] = (
        tail[...] + jnp.concatenate([jnp.zeros((8, channels), jnp.float32), back[1]])
    ).astype(dproj_ref.dtype)
    load(6).start()
    for step in steps[1:]:
        step()
    sent()

    @pl.when(me > 0)
    def _():
        home.wait_send()

    for q in (4, 5, 6):
        load(q).wait()


def recurrence_back(
    proj, halo, conv, cum, logits, o, gate, du, starts, cols, rows, taps, gain, grads
):
    n = lax.axis_size("seq")
    sizes = axis_sizes(n)
    length, channels = proj.shape
    keys = cum.shape[1]
    heads = keys // DK
    value = heads * DV
    tiles = length // TILE
    f32 = jnp.float32
    shape = jax.ShapeDtypeStruct
    depth = grads[0].shape[3]
    plan = build_plan(tuple(g.shape[4] // TILE for g in grads), SHARES, BACKWARD_PIECES, SPREAD)
    blocks = sum(g.shape[4] for g in grads) // TILE
    vmem, anywhere = pl.BlockSpec(memory_space=pltpu.VMEM), pl.BlockSpec(memory_space=pl.ANY)
    return pl.pallas_call(
        functools.partial(backward_kernel, n, sizes, plan),
        in_specs=[anywhere, vmem] + [anywhere] * 7 + [vmem] * 4 + [anywhere] * 2,
        out_specs=(anywhere,) * 3 + (vmem,) * 3,
        out_shape=(
            shape((length, channels), jnp.bfloat16),
            shape((length, value), jnp.bfloat16),
            shape((length, keys), f32),
            shape((8, channels), f32),
            shape((8, DV), f32),
            shape((blocks, depth, TILE), jnp.bfloat16),
        ),
        scratch_shapes=[
            pltpu.VMEM((length, channels), jnp.bfloat16),
            pltpu.VMEM((length, channels), f32),
            pltpu.VMEM((length, keys), f32),
            pltpu.VMEM((length, keys), f32),
            pltpu.VMEM((length, value), f32),
            pltpu.VMEM((length, value), f32),
            pltpu.VMEM((length, value), f32),
            pltpu.VMEM(starts.shape, f32),
            pltpu.VMEM((length, channels), jnp.bfloat16),
            pltpu.VMEM((length, value), jnp.bfloat16),
            pltpu.VMEM((length, keys), f32),
            pltpu.SemaphoreType.DMA((5, tiles)),
            pltpu.SemaphoreType.DMA((7,)),
            pltpu.VMEM((length, value), f32),
            pltpu.VMEM((length, channels), f32),
            pltpu.VMEM((heads, DV, DK), f32),
            pltpu.VMEM((tiles, heads, DV, DK), f32),
            pltpu.VMEM((8, channels), f32),
            pltpu.VMEM((2, 8, channels), f32),
            pltpu.VMEM((16, channels), f32),
        ]
        + chain_scratch(sizes, heads * DV // TILE, length)
        + [pltpu.SemaphoreType.DMA((2,))]
        + scatter_scratch(sizes, plan, depth, TILE, jnp.bfloat16),
        compiler_params=pltpu.CompilerParams(
            collective_id=5, has_side_effects=True, vmem_limit_bytes=60 << 20
        ),
    )(proj, halo, conv, cum, logits, o, gate, du, starts, cols, rows, taps, gain, *grads)


def tail_kernel(
    n,
    sizes,
    plan,
    shared,
    taken,
    inv_ref,
    early_ref,
    later_ref,
    dproj_ref,
    dgate_ref,
    normed_ref,
    dlogits_ref,
    lowrank_ref,
    upper_ref,
    down_ref,
    gain_ref,
    gains_two_ref,
    dtaps_ref,
    dhead_ref,
    w_ref,
    tokens_ref,
    dh_ref,
    left_ref,
    out_ref,
    small_out,
    grad_ref,
    left_out,
    grads,
    weights,
    tokens,
    dh,
    total,
    trade,
    fin,
    send,
    small,
    wide,
    narrow,
    b_sem,
    a_send,
    a_recv,
    s_send,
    s_recv,
    l_sem,
    *refs,
):
    me, core = lax.axis_index("seq"), lax.axis_index("head")
    slots, _, rows, bw = out_ref.shape
    length, width = normed_ref.shape
    channels = dproj_ref.shape[1]
    keys, rank, tap_count = dlogits_ref.shape[1], down_ref.shape[0], 4
    downs = early_ref.shape[0] - taken
    count = fin.shape[0] - 1 - early_ref.shape[0] - later_ref.shape[0]
    tiles = s_send.shape[0]
    step_rows = length // tiles
    f32 = jnp.float32
    dot = functools.partial(lax.dot_general, preferred_element_type=f32)
    enter(n, me, True)
    loads = [
        pltpu.make_async_copy(source, target, l_sem.at[1 + q])
        for q, (source, target) in enumerate(((w_ref, weights), (tokens_ref, tokens), (dh_ref, dh)))
    ]
    for load in loads:
        load.start()
    block = wide.shape[1]
    per_slot = left_ref.shape[1] // block
    total_blocks = left_ref.shape[0] * per_slot

    def basis_load(k):
        at = (k // per_slot, pl.ds(k % per_slot * block, block))
        return pltpu.make_async_copy(left_ref.at[at], wide.at[k % 2], b_sem.at[k % 2])

    def basis_store(k):
        at = (k // per_slot, pl.ds(k % per_slot * block, block))
        return pltpu.make_async_copy(narrow.at[k % 2], left_out.at[at], b_sem.at[2 + k % 2])

    pending = list(range(total_blocks))

    def narrow_basis(count):
        for k in pending[:count]:
            basis_load(k).wait()
            if k >= 2:
                basis_store(k - 2).wait()
            narrow[k % 2] = wide[k % 2].astype(narrow.dtype)
            basis_store(k).start()
            if k + 2 < total_blocks:
                basis_load(k + 2).start()
        del pending[:count]

    for k in range(min(2, total_blocks)):
        basis_load(k).start()
    steps, sent = scatter_steps(sizes, plan, [grads], refs[:-5], fin, bw, in_place=True)
    sums = sum_steps(sizes, shared, small, small_out, *refs[-5:])

    def block_grads(lo, hi):
        for source, base in ((dproj_ref, 0), (dgate_ref, channels)):
            first, last = max(lo - base, 0), min(hi - base, source.shape[1])
            if first >= last:
                continue

            part = dot(normed_ref[...], source[:, first:last], dimension_numbers=TN)
            grads[:, :, :, :, base + first : base + last] = part.astype(grads.dtype).reshape(
                sizes + (rows, last - first)
            )

    cut = max(hi for _, _, hi, _, _, group in plan if group == 0) * bw
    block_grads(0, cut)
    steps[0]()
    block_grads(cut, grads.shape[4])
    steps[1]()
    fin[fin.shape[0] - 1] = jnp.zeros(fin.shape[1:], fin.dtype)
    if taken:
        fin[count : count + taken] = early_ref[downs:]
    fin[count + taken : fin.shape[0] - 1 - downs] = later_ref[...]
    fin[fin.shape[0] - 1 - downs : fin.shape[0] - 1] = early_ref[0:downs]

    def swap(t):
        at = pl.ds(t * step_rows, step_rows)
        return pltpu.make_async_remote_copy(
            src_ref=total.at[at],
            dst_ref=trade.at[at],
            send_sem=s_send.at[t],
            recv_sem=s_recv.at[t],
            device_id={"head": 1 - core},
            device_id_type=MESH,
        )

    for load in loads:
        load.wait()
    upper = halves(upper_ref[0:rank, :])
    down_low = down_ref[...].astype(jnp.bfloat16)
    small[...] = jnp.zeros_like(small)
    upper_grad = jnp.zeros((rank, keys), f32)
    bias_grad = jnp.zeros((1, keys), f32)
    for t in range(tiles):
        at = slice(t * step_rows, (t + 1) * step_rows)
        dlogits = dlogits_ref[at, :]
        parts = halves(dlogits)
        dlow = product(parts, upper, NT).astype(jnp.bfloat16)
        upper_grad += product(halves(lowrank_ref[at, :]), parts, TN)
        bias_grad += jnp.sum(dlogits, axis=0, keepdims=True)
        small[0:rank, :] += dot(dlow, normed_ref[at, :], dimension_numbers=TN)
        part = (
            dot(dproj_ref[at, :], weights[:, :channels], dimension_numbers=NT)
            + dot(dgate_ref[at, :], weights[:, channels:], dimension_numbers=NT)
            + dot(dlow, down_low, dimension_numbers=NN)
        )
        total[at, :] = part.astype(total.dtype)
        swap(t).start()
        tok = tokens[at, :].astype(f32)
        inverse = lax.rsqrt(jnp.mean(tok * tok, axis=1, keepdims=True) + norm_epsilon)
        small[rank + 1 : rank + 2, :] += jnp.sum(part * (tok * inverse), axis=0, keepdims=True)
    small[rank : rank + 1, 0:DV] = dhead_ref[0:1, :]
    small[shared : shared + 1, :] = gains_two_ref[0:1, :]
    small[shared + 1 : shared + 1 + tap_count, :] = dtaps_ref[0:tap_count, :]
    per = width // keys
    base = shared + 1 + tap_count
    for r in range(rank + 1):
        row = bias_grad if r == rank else upper_grad[r : r + 1]
        small[base + r // per : base + r // per + 1, (r % per) * keys : (r % per + 1) * keys] = row
    sums[0]()
    narrow_basis(2)
    steps[2]()
    sums[1]()

    for t in range(tiles):
        at = slice(t * step_rows, (t + 1) * step_rows)
        swap(t).wait_recv()
        dxn = total[at, :].astype(f32) + trade[at, :].astype(f32)
        tok = tokens[at, :].astype(f32)
        inverse = lax.rsqrt(jnp.mean(tok * tok, axis=1, keepdims=True) + norm_epsilon)
        scaled = gain_ref[...] * dxn
        mean = jnp.mean(scaled * tok, axis=1, keepdims=True)
        dh[at, :] = dh[at, :] + (
            inverse * scaled - tok * (inverse * inverse * inverse * mean)
        )
    store = pltpu.make_async_copy(dh, grad_ref, l_sem.at[4])
    store.start()
    for s, step in enumerate(steps[3:]):
        narrow_basis(3)
        step()
        if s + 2 < len(sums):
            sums[s + 2]()
    for s in range(send.shape[0]):
        send[s] = fin[inv_ref[0, s]]

    def move(j):
        p = lax.rem(me + j, n)
        return remote(
            send.at[pl.ds(p * slots, slots)], out_ref.at[:, me], a_send.at[j], a_recv.at[j], p
        )

    for j in range(1, n):
        move(j).start()
    mine = pltpu.make_async_copy(
        send.at[pl.ds(me * slots, slots)], out_ref.at[:, me], l_sem.at[0]
    )
    mine.start()
    for step in sums[len(steps) - 1 :]:
        step()
    narrow_basis(len(pending))
    mine.wait()
    for j in range(1, n):
        move(j).wait()
    sent()
    for k in range(max(0, total_blocks - 2), total_blocks):
        basis_store(k).wait()
    for t in range(tiles):
        swap(t).wait_send()
    store.wait()


def tail(
    inverse, early, later, dproj, dgate, normed, dlogits, lowrank, upper, down, gain, gains_two,
    dtaps, dhead, weights, tokens, dh, left, slots, taken
):
    n = lax.axis_size("seq")
    sizes = axis_sizes(n)
    most = max(sizes)
    length, width = normed.shape
    _, rows, bw = early.shape
    columns = dproj.shape[1] + dgate.shape[1]
    blocks = columns // bw
    rank = down.shape[0]
    shared = rank + 8
    plan = build_plan((blocks,), SHARES, 3, SPREAD)
    shape = jax.ShapeDtypeStruct
    vmem, anywhere = pl.BlockSpec(memory_space=pltpu.VMEM), pl.BlockSpec(memory_space=pl.ANY)
    b16, f32 = jnp.bfloat16, jnp.float32
    small = (shared + 16, width)
    tiles = 4
    out, summed, grad, left = pl.pallas_call(
        functools.partial(tail_kernel, n, sizes, plan, shared, taken),
        out_shape=(
            shape((slots, n, rows, bw), b16),
            shape(small, f32),
            shape((length, width), f32),
            shape(left.shape, b16),
        ),
        in_specs=[pl.BlockSpec(memory_space=pltpu.SMEM)] + [vmem] * 13 + [anywhere] * 4,
        out_specs=(anywhere, vmem, anywhere, anywhere),
        scratch_shapes=[
            pltpu.VMEM(sizes + (rows, columns), b16),
            pltpu.VMEM((width, columns), b16),
            pltpu.VMEM((length, width), b16),
            pltpu.VMEM((length, width), f32),
            pltpu.VMEM((length, width), b16),
            pltpu.VMEM((length, width), b16),
            pltpu.VMEM((blocks + early.shape[0] + later.shape[0] + 1, rows, bw), b16),
            pltpu.VMEM((slots * n, rows, bw), b16),
            pltpu.VMEM(small, f32),
            pltpu.VMEM((2, width // 4, width), f32),
            pltpu.VMEM((2, width // 4, width), b16),
            pltpu.SemaphoreType.DMA((4,)),
            pltpu.SemaphoreType.DMA((n,)),
            pltpu.SemaphoreType.DMA((n,)),
            pltpu.SemaphoreType.DMA((tiles,)),
            pltpu.SemaphoreType.DMA((tiles,)),
            pltpu.SemaphoreType.DMA((5,)),
        ]
        + scatter_scratch(sizes, plan, rows, bw, b16, in_place=True)
        + [
            pltpu.VMEM((shared, width), f32),
            pltpu.VMEM((3,) + small, f32),
            pltpu.VMEM((3, most) + small, f32),
            pltpu.SemaphoreType.DMA((1 + 3 * most,)),
            pltpu.SemaphoreType.DMA((1 + 3 * most,)),
        ],
        compiler_params=pltpu.CompilerParams(
            collective_id=2, has_side_effects=True, vmem_limit_bytes=60 << 20
        ),
    )(
        inverse, early, later, dproj, dgate, normed, dlogits, lowrank, upper, down, gain, gains_two,
        dtaps, dhead, weights, tokens, dh, left
    )
    return out.reshape(slots, width, bw), summed, grad, left


def adam_kernel(
    rates,
    rank,
    taps,
    grad_ref,
    left_ref,
    right_ref,
    master_ref,
    first_ref,
    second_ref,
    summed_ref,
    *refs,
):
    params = [refs[3 * q : 3 * q + 3] for q in range(5)]
    grad_in, result_in = refs[15:17]
    grad_out, master_out, first_out, second_out, copy_out = refs[17:22]
    news = [refs[22 + 4 * q : 26 + 4 * q] for q in range(5)]
    grad_pass, result_ref = refs[42:]
    grad_pass[...] = grad_in[...]
    result_ref[...] = result_in[...]

    @pl.when(pl.program_id(0) == 0)
    def _():
        shared = rank + 8
        width = summed_ref.shape[1]
        keys = news[2][0].shape[1]
        per = width // keys
        base = shared + 1 + taps
        gains, down, upper, head, conv = news
        gains[0][0:1, :] = summed_ref[rank + 1 : rank + 2, :]
        gains[0][1:2, :] = summed_ref[shared : shared + 1, :]
        down[0][...] = summed_ref[0:rank, :]
        for r in range(rank + 1):
            upper[0][r : r + 1, :] = summed_ref[
                base + r // per : base + r // per + 1, (r % per) * keys : (r % per + 1) * keys
            ]
        head[0][...] = summed_ref[rank : rank + 1, 0:DV]
        conv[0][...] = summed_ref[shared + 1 : shared + 1 + taps, :]
        for (value, first, second), new, rate in zip(params, news, rates, strict=True):
            new[1][...], new[2][...], new[3][...] = plain_adam(
                value[...], new[0][...], first[...], second[...], rate
            )

    width = left_ref.shape[1]
    step = min(256, width)
    dot = functools.partial(
        lax.dot_general, dimension_numbers=TN, preferred_element_type=jnp.float32
    )
    grad_out[0] = grad_ref[0].astype(jnp.float32)
    left = left_ref[0]
    dot = functools.partial(lax.dot_general, preferred_element_type=jnp.float32)
    right = halves(right_ref[0])
    rotated = dot(left, grad_ref[0], dimension_numbers=TN)
    rotated = product(halves(rotated), right, NN)
    first = moment_decay * first_ref[0] + (1.0 - moment_decay) * rotated
    second = moment_decay * second_ref[0] + (1.0 - moment_decay) * rotated * rotated
    first_out[0] = first
    second_out[0] = second
    direction = first / (jnp.sqrt(second) + adam_epsilon)
    turned = product(halves(direction), right, NT).astype(left.dtype)
    master = master_ref[0] - rate_block * dot(left, turned, dimension_numbers=NN)
    master_out[0] = master
    copy_out[0] = master.astype(copy_out.dtype)


def all_adam(grads, left, right, master, first, second, summed, params, grad, result):
    slots, width, columns = master.shape
    tall = pl.BlockSpec((1, width, columns), lambda i: (i, 0, 0))
    length, model = grad.shape
    wide = pl.BlockSpec((length // slots, model), lambda i: (i, 0))
    shape = jax.ShapeDtypeStruct
    full = shape(master.shape, jnp.float32)

    def whole(array):
        return pl.BlockSpec(array.shape, lambda i: (0, 0))

    flat = [array for triple in params for array in triple]
    rates = (rate_gains, rate_down, rate_upper, rate_head, rate_conv)
    news = [triple[0] for triple in params for _ in range(4)]
    return pl.pallas_call(
        functools.partial(adam_kernel, rates, params[1][0].shape[0], params[4][0].shape[0]),
        grid=(slots,),
        out_shape=tuple(
            [full] * 4
            + [shape(master.shape, jnp.bfloat16)]
            + [shape(new.shape, new.dtype) for new in news]
            + [shape(grad.shape, jnp.float32), shape(grad.shape, jnp.bfloat16)]
        ),
        in_specs=[
            tall,
            pl.BlockSpec((1, width, width), lambda i: (i, 0, 0)),
            pl.BlockSpec((1, columns, columns), lambda i: (i, 0, 0)),
            tall,
            tall,
            tall,
            whole(summed),
        ]
        + [whole(array) for array in flat]
        + [wide] * 2,
        out_specs=[tall] * 5 + [whole(new) for new in news] + [wide] * 2,
        compiler_params=pltpu.CompilerParams(vmem_limit_bytes=56 << 20),
    )(grads, left, right, master, first, second, summed, *flat, grad, result)


def middle_kernel(
    n,
    sizes,
    plan,
    u_ref,
    w_out_ref,
    cols_ref,
    gain_ref,
    tokens_ref,
    w_up_ref,
    w_down_ref,
    cot_ref,
    early_ref,
    sum_ref,
    result_out,
    dh_out,
    du_out,
    g_up_out,
    g_out_out,
    w_up,
    w_down,
    mixed,
    hidden_sum,
    normed,
    inv,
    dy,
    hid,
    dpair,
    send,
    recv,
    g_down,
    g_up,
    g_out,
    du,
    free,
    s_sem,
    r_sem,
    l_sem,
    *scatter_refs,
):
    me, core = lax.axis_index("seq"), lax.axis_index("head")
    length, width = normed.shape
    inner = hid.shape[1]
    rows = g_out.shape[3]
    f32 = jnp.float32
    dot = functools.partial(lax.dot_general, preferred_element_type=f32)
    tiles = s_sem.shape[0] // 3
    block = length // tiles
    ats = [slice(t * block, (t + 1) * block) for t in range(tiles)]
    enter(n, me, True)
    loads = [
        pltpu.make_async_copy(source, target, l_sem.at[q])
        for q, (source, target) in enumerate(
            ((tokens_ref, mixed), (w_up_ref, w_up), (w_down_ref, w_down), (cot_ref, dy))
        )
    ]
    for load in loads:
        load.start()
    flushes = []

    def flush(source, target):
        copy = pltpu.make_async_copy(source, target, l_sem.at[4 + len(flushes)])
        copy.start()
        flushes.append(copy)

    steps, sent = scatter_steps(
        sizes, plan, [g_down, g_up], scatter_refs, early_ref, TILE, in_place=True
    )

    def advance(count=1):
        for step in steps[:count]:
            step()
        del steps[:count]

    def swap(phase, t):
        at = pl.ds(t * block, block)
        return pltpu.make_async_remote_copy(
            src_ref=send.at[at],
            dst_ref=recv.at[at],
            send_sem=s_sem.at[phase * tiles + t],
            recv_sem=r_sem.at[phase * tiles + t],
            device_id={"head": 1 - core},
            device_id_type=MESH,
        )

    def exchange(phase, left, right, close):
        if phase:
            for t in range(tiles):
                swap(phase - 1, t).wait_send()
            pl.semaphore_wait(free, 1)
        for t, at in enumerate(ats):
            send[at, :] = dot(left[at, :], right[...], dimension_numbers=NT).astype(send.dtype)
            swap(phase, t).start()
            if t:
                swap(phase, t - 1).wait_recv()
                close(ats[t - 1])
        swap(phase, tiles - 1).wait_recv()
        close(ats[-1])
        if phase < 2:
            pl.semaphore_signal(
                free, inc=1, device_id={"head": 1 - core}, device_id_type=MESH
            )

    def both(at):
        return send[at, :].astype(f32) + recv[at, :].astype(f32)

    loads[0].wait()

    def close_attn(at):
        total = mixed[at, :].astype(f32) + both(at)
        inverse = lax.rsqrt(jnp.mean(total * total, axis=1, keepdims=True) + norm_epsilon)
        hidden_sum[at, :] = total
        inv[at, :] = inverse
        normed[at, :] = (total * inverse * gain_ref[...]).astype(normed.dtype)

    exchange(0, u_ref, w_out_ref, close_attn)
    for load in loads[1:]:
        load.wait()

    def feed(t, _):
        at = pl.ds(pl.multiple_of(t * block, block), block)
        x = normed[at, :]
        grad_y = (dy[at, :].astype(f32) * cols_ref[at, 7:8]).astype(dy.dtype)
        dy[at, :] = grad_y
        for lo in range(0, inner, 512):
            hi = min(lo + 512, inner)
            gate = dot(x, w_up[:, lo:hi], dimension_numbers=NN)
            up = dot(x, w_up[:, inner + lo : inner + hi], dimension_numbers=NN)
            grad = dot(grad_y, w_down[:, lo:hi], dimension_numbers=NN)
            sig = sigmoid(gate)
            swish = gate * sig
            hid[at, lo:hi] = (swish * up).astype(hid.dtype)
            dpair[at, lo:hi] = (grad * up * (sig + swish * (1.0 - sig))).astype(dpair.dtype)
            dpair[at, inner + lo : inner + hi] = (grad * swish).astype(dpair.dtype)
        return 0

    lax.fori_loop(0, tiles, feed, 0)

    def block_grads(left, source, target, lo, hi):
        for first in range(lo, hi, 512):
            last = min(first + 512, hi)
            part = dot(left[...], source[:, first:last], dimension_numbers=TN)
            target[:, :, :, :, first:last] = part.astype(target.dtype).reshape(
                sizes + (rows, last - first)
            )

    block_grads(dy, hid, g_down, 0, inner)
    advance()
    block_grads(normed, dpair, g_up, 0, inner)
    advance()
    block_grads(normed, dpair, g_up, inner, 2 * inner)
    taken = g_up.shape[4] - g_up_out.shape[4]
    flush(g_up.at[:, :, :, :, pl.ds(taken, g_up_out.shape[4])], g_up_out)

    def close_mlp(at):
        mixed[at, :] = (hidden_sum[at, :] + both(at)).astype(mixed.dtype)

    exchange(1, hid, w_down, close_mlp)
    flush(mixed, result_out)
    advance()

    sum_ref[...] = jnp.zeros_like(sum_ref)

    def close_back(at):
        grad = both(at)
        total, inverse = hidden_sum[at, :], inv[at, :]
        unit = total * inverse
        scaled = gain_ref[...] * grad
        mean = jnp.mean(scaled * total, axis=1, keepdims=True)
        dh = dy[at, :].astype(f32) + (inverse * scaled - unit * (inverse * inverse * mean))
        hidden_sum[at, :] = dh
        normed[at, :] = dh.astype(normed.dtype)
        sum_ref[0:1, :] += jnp.sum(grad * unit, axis=0, keepdims=True)
        du[at, :] = dot(normed[at, :], w_out_ref[...], dimension_numbers=NN)

    exchange(2, dpair, w_up, close_back)
    flush(hidden_sum, dh_out)
    flush(du, du_out)
    advance()
    block_grads(normed, u_ref, g_out, 0, u_ref.shape[1])
    flush(g_out, g_out_out)
    advance(len(steps))
    sent()
    for t in range(tiles):
        swap(2, t).wait_send()
    for copy in flushes:
        copy.wait()


def middle(u, w_out, cols, gain, tokens, w_up, w_down, cot, taken):
    n = lax.axis_size("seq")
    sizes = axis_sizes(n)
    length, width = tokens.shape
    value, inner = u.shape[1], w_down.shape[1]
    rows = width // n
    f32, b16 = jnp.float32, jnp.bfloat16
    blocks = inner // TILE
    plan = build_plan((blocks, taken) if taken else (blocks,), SHARES, MIDDLE_PIECES, SPREAD)
    shape = jax.ShapeDtypeStruct
    vmem, anywhere = pl.BlockSpec(memory_space=pltpu.VMEM), pl.BlockSpec(memory_space=pl.ANY)
    tiles = 4
    return pl.pallas_call(
        functools.partial(middle_kernel, n, sizes, plan),
        out_shape=(
            shape((blocks + taken, rows, TILE), b16),
            shape((8, width), f32),
            shape((length, width), b16),
            shape((length, width), f32),
            shape((length, value), f32),
            shape(sizes + (rows, 2 * inner - taken * TILE), b16),
            shape(sizes + (rows, value), b16),
        ),
        in_specs=[vmem] * 4 + [anywhere] * 4,
        out_specs=(vmem, vmem) + (anywhere,) * 5,
        scratch_shapes=[
            pltpu.VMEM((width, 2 * inner), b16),
            pltpu.VMEM((width, inner), b16),
            pltpu.VMEM((length, width), b16),
            pltpu.VMEM((length, width), f32),
            pltpu.VMEM((length, width), b16),
            pltpu.VMEM((length, 1), f32),
            pltpu.VMEM((length, width), b16),
            pltpu.VMEM((length, inner), b16),
            pltpu.VMEM((length, 2 * inner), b16),
            pltpu.VMEM((length, width), b16),
            pltpu.VMEM((length, width), b16),
            pltpu.VMEM(sizes + (rows, inner), b16),
            pltpu.VMEM(sizes + (rows, 2 * inner), b16),
            pltpu.VMEM(sizes + (rows, value), b16),
            pltpu.VMEM((length, value), f32),
            pltpu.SemaphoreType.REGULAR,
            pltpu.SemaphoreType.DMA((3 * tiles,)),
            pltpu.SemaphoreType.DMA((3 * tiles,)),
            pltpu.SemaphoreType.DMA((9,)),
        ]
        + scatter_scratch(sizes, plan, rows, TILE, b16, in_place=True),
        compiler_params=pltpu.CompilerParams(
            collective_id=6, has_side_effects=True, vmem_limit_bytes=62 << 20
        ),
    )(u, w_out, cols, gain, tokens, w_up, w_down, cot)


def plain_adam(param, gradient, first, second, rate):
    first_next = moment_decay * first + (1.0 - moment_decay) * gradient
    second_next = moment_decay * second + (1.0 - moment_decay) * gradient * gradient
    return (
        param - rate * first_next / (jnp.sqrt(second_next) + adam_epsilon),
        first_next,
        second_next,
    )


def body(
    tokens,
    cotangent,
    lengths,
    packing,
    owners,
    slot_copy,
    slot_master,
    slot_first,
    slot_second,
    basis_left,
    basis_right,
    norm_gains,
    gains_first,
    gains_second,
    gate_down,
    down_first,
    down_second,
    gate_up,
    upper_first,
    upper_second,
    head_gain,
    head_first,
    head_second,
    conv_weight,
    conv_first,
    conv_second,
):
    tok_rows = tokens.shape[0]
    model_width = tokens.shape[1]
    block_width = slot_copy.shape[2]
    tap_count = conv_weight.shape[0]
    key_width = gate_up.shape[1]
    channels = conv_weight.shape[1]
    value_width = channels - 2 * key_width
    block_total = owners.shape[1]
    count_in = (channels + value_width) // block_width
    count_out = value_width // block_width
    count_down = (block_total - count_in - count_out) // 3
    count_up = 2 * count_down
    (in_weights, up_weights, out_weights, down_weights), kept = forward(
        owners,
        lengths,
        packing,
        slot_copy,
        tokens,
        norm_gains[0:1],
        gate_down.T,
        gate_up,
        conv_weight,
        head_gain[None],
        (count_in, count_up, count_out, count_down),
    )
    normed, lowrank, logits, mixed_proj, halo, gate_pre = kept[:6]
    conv_pre, cumulative, attended, gated_out, starts, cols, rows = kept[6:]
    gain_row = head_gain[None]
    early, gains_two, result, grad_one, grad_gated, grad_up, grad_out = middle(
        gated_out,
        out_weights,
        cols,
        norm_gains[1:2],
        tokens,
        up_weights,
        down_weights,
        cotangent,
        MIDDLE_TAKEN,
    )
    grad_mixed, grad_gate_pre, grad_logits, tap_grads, gain_grads, later = recurrence_back(
        mixed_proj,
        halo,
        conv_pre,
        cumulative,
        logits,
        attended,
        gate_pre,
        grad_gated,
        starts,
        cols,
        rows,
        conv_weight,
        gain_row,
        (grad_up, grad_out),
    )
    slots_dev = slot_copy.shape[0]
    slot_total = slots_dev * lax.axis_size("seq")
    named = jnp.arange(slot_total, dtype=jnp.int32)[:, None] == owners
    inverse = jnp.where(
        jnp.any(named, axis=1),
        jnp.sum(named * jnp.arange(block_total, dtype=jnp.int32), axis=1),
        block_total,
    ).astype(jnp.int32)[None]
    owned_grads, summed, grad_input, left_low = tail(
        inverse,
        early,
        later,
        grad_mixed,
        grad_gate_pre,
        normed,
        grad_logits,
        lowrank,
        gate_up,
        gate_down.T,
        norm_gains[0:1],
        gains_two,
        tap_grads,
        gain_grads,
        in_weights,
        tokens,
        grad_one,
        basis_left,
        slots_dev,
        MIDDLE_TAKEN,
    )
    params = (
        (norm_gains, gains_first, gains_second),
        (gate_down.T, down_first.T, down_second.T),
        (gate_up, upper_first, upper_second),
        (head_gain[None], head_first[None], head_second[None]),
        (conv_weight, conv_first, conv_second),
    )
    (
        owned_grads,
        master_next,
        first_next,
        second_next,
        copy_next,
        *small_next,
        grad_input,
        result,
    ) = all_adam(
        owned_grads,
        left_low,
        basis_right,
        slot_master,
        slot_first,
        slot_second,
        summed,
        params,
        grad_input,
        result,
    )
    for q in range(4, 8):
        small_next[q] = small_next[q].T
    for q in range(12, 16):
        small_next[q] = small_next[q][0]
    return (
        result,
        grad_input,
        owned_grads,
        master_next,
        first_next,
        second_next,
        copy_next,
        *small_next,
    )


def solution(mesh):
    placed = (
        P("seq", None),
        P("seq", None),
        P(),
        P(),
        P("head", None),
        P(("seq", "head"), None, None),
        P(("seq", "head"), None, None),
        P(("seq", "head"), None, None),
        P(("seq", "head"), None, None),
        P(("seq", "head"), None, None),
        P(("seq", "head"), None, None),
        P(),
        P(),
        P(),
        P(),
        P(),
        P(),
        P(None, "head"),
        P(None, "head"),
        P(None, "head"),
        P(),
        P(),
        P(),
        P(None, "head"),
        P(None, "head"),
        P(None, "head"),
    )
    return jax.shard_map(
        body,
        mesh=mesh,
        in_specs=placed,
        out_specs=(
            P("seq", None),
            P("seq", None),
            P(("seq", "head"), None, None),
            P(("seq", "head"), None, None),
            P(("seq", "head"), None, None),
            P(("seq", "head"), None, None),
            P(("seq", "head"), None, None),
            P(),
            P(),
            P(),
            P(),
            P(),
            P(),
            P(),
            P(),
            P(None, "head"),
            P(None, "head"),
            P(None, "head"),
            P(None, "head"),
            P(),
            P(),
            P(),
            P(),
            P(None, "head"),
            P(None, "head"),
            P(None, "head"),
            P(None, "head"),
        ),
        check_vma=False,
    )
```

profile of v0, /device:TPU:30, one launch (start us, length us, event | category | flops | bytes accessed | tf_op | source)
XLA Modules:
  0.0 420.8 jit_solution(18345395724243443910)
XLA Ops:
  0.7 1.4 fusion.1
  2.0 156.7 %shard_map.457 = (bf16[4,2,2,64,1536]{4,3,2,1,0:T(8,128)(2,1)}, bf16[4,2,2,64,2816]{4,3,2,1,0:T(8,128)(2,1)}, bf16[4,2,2,64,512]{4,3,2,1,0:T(8,128)(2,1)}, bf16[...) custom-call(s32[1,49]{1,0:T(1,128)} %owners_ref.1, ...), custom_call_target="tpu_custom_call" | custom-call | tf_op jit(solution)/shard_map/pallas_call | solution.py:947
  158.7 81.0 %shard_map.458 = (bf16[17,64,128]{2,1,0:T(8,128)(2,1)}, f32[8,1024]{1,0:T(8,128)}, bf16[1024,1024]{1,0:T(8,128)(2,1)}, f32[1024,1024]{1,0:T(8,128)}, f32[1024,51...) custom-call(bf16[1024,512]{1,0:T(8,128)(2,1)} %get-tuple-element.88.u_ref, ...), custom_call_target="tpu_custom_call" | custom-call | tf_op jit(solution)/shard_map/pallas_call | solution.py:1947
  239.7 0.0 copy-start
  239.7 77.7 %shard_map.459 = (bf16[1024,1024]{1,0:T(8,128)(2,1)}, bf16[1024,512]{1,0:T(8,128)(2,1)}, f32[1024,256]{1,0:T(8,128)}, f32[8,1024]{1,0:T(8,128)}, f32[8,256]{1,0:T(8,128)}, /*index=5*/bf16[20,64,128]{2,1,0:T(8,128)(2,1)}) custom-call(bf16[1024,1024]{1,0:T(8,128)(2,1)} %get-tuple-element.94.proj_in, bf16[16,1024]{1,0:T(8,128)(2,1)} %get-tuple-element.95.halo_ref, ...), custom_call_target="tpu_custom_call" | custom-call | tf_op jit(solution)/shard_map/pallas_call | solution.py:1320
  317.4 0.0 copy-done
  317.4 0.1 fusion
  317.5 0.1 select_reduce_fusion
  317.6 0.5 select_bitcast_fusion.inv_ref
  318.1 83.6 %shard_map.460 = (bf16[4,16,64,128]{3,2,1,0:T(8,128)(2,1)}, f32[40,1024]{1,0:T(8,128)}, f32[1024,1024]{1,0:T(8,128)}, bf16[4,1024,1024]{2,1,0:T(8,128)(2,1)}) custom-call(s32[1,64]{1,0:T(1,128)} %select_bitcast_fusion.inv_ref, bf16[17,64,128]{2,1,0:T(8,128)(2,1)} %get-tuple-element.93.early_ref, bf16[20,64,128]{2,1,0:T(8,128)(2,1)} %get-tuple-element.106.later_ref, ...), custom_call_target="tpu_custom_call" | custom-call | tf_op jit(solution)/shard_map/pallas_call | solution.py:1595
  401.7 18.8 %shard_map.461 = (f32[4,1024,128]{2,1,0:T(8,128)}, f32[4,1024,128]{2,1,0:T(8,128)}, f32[4,1024,128]{2,1,0:T(8,128)}, f32[4,1024,128]{2,1,0:T(8,128)}, bf16[4,102...) custom-call(bf16[4,1024,128]{2,1,0:T(8,128)(2,1)} %bitcast.26, ...), custom_call_target="tpu_custom_call" | custom-call | tf_op jit(solution)/shard_map/pallas_call | solution.py:1721
Async XLA Ops:
  239.7 77.7 %copy-start = (s32[1,49]{1,0:T(1,128)S(1)}, s32[1,49]{1,0:T(1,128)}, u32[]{:S(2)}) copy-start(s32[1,49]{1,0:T(1,128)} %owners_ref.1) | copy-start | bytes 592
where the time goes:
time: 425 us; the launch traced here: 421 us
  Pallas kernels  418 us (98%)
    pallas_call x1, Pallas kernels, forward(): pl.pallas_call(functools.partial(forward_kernel, n, sizes, plan, ready),...  157 us
    pallas_call x1, Pallas kernels, tail(): pl.pallas_call(functools.partial(tail_kernel, n, sizes, plan, shared, tak...  83.6 us
    pallas_call x1, Pallas kernels, middle(): pl.pallas_call(functools.partial(middle_kernel, n, sizes, plan), out_shap...  81 us
    pallas_call x1, Pallas kernels, recurrence_back(): pl.pallas_call(functools.partial(backward_kernel, n, sizes, plan), in_spe...  77.7 us
    pallas_call x1, Pallas kernels, all_adam(): pl.pallas_call(functools.partial(adam_kernel, rates, params[1][0].shape[0...  18.8 us

commit v1 on v0

--- a/solution.py
+++ b/solution.py
@@ -49,7 +49,7 @@
     return index_of(d, sizes)
 
 
-def enter(n, me, mate=False):
+def announce(n, me, mate=False):
     barrier = pltpu.get_barrier_semaphore()
     if mate:
         core = lax.axis_index("head")
@@ -58,7 +58,11 @@
         pl.semaphore_signal(
             barrier, inc=1, device_id={"seq": lax.rem(me + j, n)}, device_id_type=MESH
         )
-    pl.semaphore_wait(barrier, n - 1 + int(mate))
+
+
+def enter(n, me, mate=False):
+    announce(n, me, mate)
+    pl.semaphore_wait(pltpu.get_barrier_semaphore(), n - 1 + int(mate))
 
 
 def remote(src, dst, send_sem, recv_sem, peer):
@@ -683,7 +687,7 @@
     def norm(values):
         values = values.astype(jnp.float32)
         inverse = lax.rsqrt(jnp.mean(values * values, axis=1, keepdims=True) + norm_epsilon)
-        return (values * inverse * norm_ref[...]).astype(jnp.bfloat16)
+        return (values * inverse * norm_ref[0:1, :]).astype(jnp.bfloat16)
 
     i = lax.broadcasted_iota(jnp.int32, (TILE, TILE), 0)
     j = lax.broadcasted_iota(jnp.int32, (TILE, TILE), 1)
@@ -1418,7 +1422,7 @@
     step_rows = length // tiles
     f32 = jnp.float32
     dot = functools.partial(lax.dot_general, preferred_element_type=f32)
-    enter(n, me, True)
+    announce(n, me, True)
     loads = [
         pltpu.make_async_copy(source, target, l_sem.at[1 + q])
         for q, (source, target) in enumerate(((w_ref, weights), (tokens_ref, tokens), (dh_ref, dh)))
@@ -1468,6 +1472,7 @@
 
     cut = max(hi for _, _, hi, _, _, group in plan if group == 0) * bw
     block_grads(0, cut)
+    pl.semaphore_wait(pltpu.get_barrier_semaphore(), n)
     steps[0]()
     block_grads(cut, grads.shape[4])
     steps[1]()
@@ -1532,7 +1537,7 @@
         dxn = total[at, :].astype(f32) + trade[at, :].astype(f32)
         tok = tokens[at, :].astype(f32)
         inverse = lax.rsqrt(jnp.mean(tok * tok, axis=1, keepdims=True) + norm_epsilon)
-        scaled = gain_ref[...] * dxn
+        scaled = gain_ref[0:1, :] * dxn
         mean = jnp.mean(scaled * tok, axis=1, keepdims=True)
         dh[at, :] = dh[at, :] + (
             inverse * scaled - tok * (inverse * inverse * inverse * mean)
@@ -1856,7 +1861,7 @@
         inverse = lax.rsqrt(jnp.mean(total * total, axis=1, keepdims=True) + norm_epsilon)
         hidden_sum[at, :] = total
         inv[at, :] = inverse
-        normed[at, :] = (total * inverse * gain_ref[...]).astype(normed.dtype)
+        normed[at, :] = (total * inverse * gain_ref[1:2, :]).astype(normed.dtype)
 
     exchange(0, u_ref, w_out_ref, close_attn)
     for load in loads[1:]:
@@ -1910,7 +1915,7 @@
         grad = both(at)
         total, inverse = hidden_sum[at, :], inv[at, :]
         unit = total * inverse
-        scaled = gain_ref[...] * grad
+        scaled = gain_ref[1:2, :] * grad
         mean = jnp.mean(scaled * total, axis=1, keepdims=True)
         dh = dy[at, :].astype(f32) + (inverse * scaled - unit * (inverse * inverse * mean))
         hidden_sum[at, :] = dh
@@ -2041,7 +2046,7 @@
         packing,
         slot_copy,
         tokens,
-        norm_gains[0:1],
+        norm_gains,
         gate_down.T,
         gate_up,
         conv_weight,
@@ -2055,7 +2060,7 @@
         gated_out,
         out_weights,
         cols,
-        norm_gains[1:2],
+        norm_gains,
         tokens,
         up_weights,
         down_weights,
@@ -2097,7 +2102,7 @@
         lowrank,
         gate_up,
         gate_down.T,
-        norm_gains[0:1],
+        norm_gains,
         gains_two,
         tap_grads,
         gain_grads,

time: 425 us -> 423 us (level)
  no operation moved by 1% of the time
where the time goes in v1:
time: 423 us; the launch traced here: 419 us
  Pallas kernels  417 us (99%)
    pallas_call x1, Pallas kernels, forward(): pl.pallas_call(functools.partial(forward_kernel, n, sizes, plan, ready),...  157 us
    pallas_call x1, Pallas kernels, tail(): pl.pallas_call(functools.partial(tail_kernel, n, sizes, plan, shared, tak...  82.5 us
    pallas_call x1, Pallas kernels, middle(): pl.pallas_call(functools.partial(middle_kernel, n, sizes, plan), out_shap...  81 us
    pallas_call x1, Pallas kernels, recurrence_back(): pl.pallas_call(functools.partial(backward_kernel, n, sizes, plan), in_spe...  77.8 us
    pallas_call x1, Pallas kernels, all_adam(): pl.pallas_call(functools.partial(adam_kernel, rates, params[1][0].shape[0...  18.8 us

profile of v1, /device:TPU:30, one launch (start us, length us, event | category | flops | bytes accessed | tf_op | source)
XLA Modules:
  0.0 418.5 jit_solution(1536764134296285672)
XLA Ops:
  0.7 156.7 %shard_map.457 = (bf16[4,2,2,64,1536]{4,3,2,1,0:T(8,128)(2,1)}, bf16[4,2,2,64,2816]{4,3,2,1,0:T(8,128)(2,1)}, bf16[4,2,2,64,512]{4,3,2,1,0:T(8,128)(2,1)}, bf16[...) custom-call(s32[1,49]{1,0:T(1,128)} %owners_ref.1, ...), custom_call_target="tpu_custom_call" | custom-call | tf_op jit(solution)/shard_map/pallas_call | solution.py:951
  157.4 81.0 %shard_map.458 = (bf16[17,64,128]{2,1,0:T(8,128)(2,1)}, f32[8,1024]{1,0:T(8,128)}, bf16[1024,1024]{1,0:T(8,128)(2,1)}, f32[1024,1024]{1,0:T(8,128)}, f32[1024,51...) custom-call(bf16[1024,512]{1,0:T(8,128)(2,1)} %get-tuple-element.88.u_ref, ...), custom_call_target="tpu_custom_call" | custom-call | tf_op jit(solution)/shard_map/pallas_call | solution.py:1952
  238.4 0.0 copy-start
  238.4 77.8 %shard_map.459 = (bf16[1024,1024]{1,0:T(8,128)(2,1)}, bf16[1024,512]{1,0:T(8,128)(2,1)}, f32[1024,256]{1,0:T(8,128)}, f32[8,1024]{1,0:T(8,128)}, f32[8,256]{1,0:T(8,128)}, /*index=5*/bf16[20,64,128]{2,1,0:T(8,128)(2,1)}) custom-call(bf16[1024,1024]{1,0:T(8,128)(2,1)} %get-tuple-element.94.proj_in, bf16[16,1024]{1,0:T(8,128)(2,1)} %get-tuple-element.95.halo_ref, ...), custom_call_target="tpu_custom_call" | custom-call | tf_op jit(solution)/shard_map/pallas_call | solution.py:1324
  316.2 0.0 copy-done
  316.2 0.1 fusion
  316.3 0.1 select_reduce_fusion
  316.4 0.5 select_bitcast_fusion.inv_ref
  316.9 82.5 %shard_map.460 = (bf16[4,16,64,128]{3,2,1,0:T(8,128)(2,1)}, f32[40,1024]{1,0:T(8,128)}, f32[1024,1024]{1,0:T(8,128)}, bf16[4,1024,1024]{2,1,0:T(8,128)(2,1)}) custom-call(s32[1,64]{1,0:T(1,128)} %select_bitcast_fusion.inv_ref, bf16[17,64,128]{2,1,0:T(8,128)(2,1)} %get-tuple-element.93.early_ref, bf16[20,64,128]{2,1,0:T(8,128)(2,1)} %get-tuple-element.106.later_ref, ...), custom_call_target="tpu_custom_call" | custom-call | tf_op jit(solution)/shard_map/pallas_call | solution.py:1600
  399.4 18.8 %shard_map.461 = (f32[4,1024,128]{2,1,0:T(8,128)}, f32[4,1024,128]{2,1,0:T(8,128)}, f32[4,1024,128]{2,1,0:T(8,128)}, f32[4,1024,128]{2,1,0:T(8,128)}, bf16[4,102...) custom-call(bf16[4,1024,128]{2,1,0:T(8,128)(2,1)} %bitcast.26, ...), custom_call_target="tpu_custom_call" | custom-call | tf_op jit(solution)/shard_map/pallas_call | solution.py:1726
Async XLA Ops:
  238.4 77.8 %copy-start = (s32[1,49]{1,0:T(1,128)S(1)}, s32[1,49]{1,0:T(1,128)}, u32[]{:S(2)}) copy-start(s32[1,49]{1,0:T(1,128)} %owners_ref.1) | copy-start | bytes 592
